TPU v7x, 32 devices: a whole 2x2x4 slice. The times are simulated.
32 devices in a mesh: seq: 32 (over z, y, x, core).
Axes of the slice: x: 2, y: 2, z: 4, core: 2. Of those that a mesh axis runs over, the one named last changes fastest.
Arguments:
- tokens: bfloat16 [4, 2048, 1024], P(None, 'seq'), may hold values from -6 to 6
- gain_attn: float32 [1024], replicated, may hold values from 0.25 to 1.75
- gain_mlp: float32 [1024], replicated, may hold values from 0.25 to 1.75
- w_query: bfloat16 [1024, 1024], replicated, may hold values from -0.1875 to 0.1875
- w_key: bfloat16 [1024, 1024], replicated, may hold values from -0.1875 to 0.1875
- w_value: bfloat16 [1024, 1024], replicated, may hold values from -0.1875 to 0.1875
- w_out: bfloat16 [1024, 1024], replicated, may hold values from -1 to 1
- w_gate: bfloat16 [1024, 2752], replicated, may hold values from -0.1875 to 0.1875
- w_up: bfloat16 [1024, 2752], replicated, may hold values from -0.1875 to 0.1875
- w_down: bfloat16 [2752, 1024], replicated, may hold values from -0.109375 to 0.109375
- cotangent: bfloat16 [4, 2048, 1024], P(None, 'seq'), may hold values from -6 to 6
- lengths: int32 [4, 8], replicated, may hold values from 192 to 320, as said below
Outputs:
- output: bfloat16 [4, 2048, 1024], P(None, 'seq')
- input_grad: float32 [4, 2048, 1024], P(None, 'seq')
- grad_gain_attn: float32 [1024], replicated
- grad_gain_mlp: float32 [1024], replicated
- grad_w_query: float32 [1048576], P('seq')
- grad_w_key: float32 [1048576], P('seq')
- grad_w_value: float32 [1048576], P('seq')
- grad_w_out: float32 [1048576], P('seq')
- grad_w_gate: float32 [2818048], P('seq')
- grad_w_up: float32 [2818048], P('seq')
- grad_w_down: float32 [2818048], P('seq')
Inputs may be any that keep to these rules, and one draw needn't show every extreme that they name: `lengths`: each row sums to 2048; every row holds a length of 192 and one of 320.
All inputs are finite; a program needn't handle non-finite values.
Results may differ from a plain program's by a relative error of at most 0.013.
Values may be sent and summed in bfloat16 or wider, within the bound.
A program may use at most 320 MiB of HBM per device.

v0:
```python
import functools
import math

import jax
import jax.numpy as jnp
from jax import lax
from jax.experimental import pallas as pl
from jax.experimental.pallas import tpu as pltpu
from jax.sharding import PartitionSpec as P

HEAD = 64
WIN = 64
EPSILON = 1e-05
MESH = pl.DeviceIdType.MESH
MOST_GROUPS = 32
CHUNK = 256
BF16 = jnp.bfloat16
F32 = jnp.float32

MATRICES = {
    "down": (("hidden", "cot"),),
    "gate": (("second", "dgate"),),
    "up": (("second", "dup"),),
    "query": (("first", "dquery"),),
    "keyval": (("first", "dkeyval"), ("before", "dkvback")),
    "out": (("attended", "branch"),),
}
ROWS = ("first", "before", "attended", "second", "hidden")
CHUNKED = ("dgate", "dup")
COLS = ("cot", "dgate", "dup", "branch", "dquery", "dkeyval", "dkvback")
PARTS = {
    "gate": ("gate", 0, 1, (2, 1, 4, 3), (1, 2, 4, 4)),
    "gate2": ("gate", 1, 11, (1, 2, 4, 3), (1, 1, 2, 2)),
    "up": ("up", 0, 4, (3, 4, 1, 2), (1, 2, 4, 4)),
    "up2": ("up", 4, 11, (2, 3, 4, 1), (1, 1, 2, 4)),
    "down": ("down", 0, 3, (3, 1, 2, 4), (1, 1, 1, 1)),
    "rest": ("down", 3, 4, (1, 2, 3, 4), (1, 1, 1, 1)),
    "out": ("out", 0, 4, (2, 1, 3, 4), (1, 1, 2, 2)),
    "query": ("query", 0, 4, (2, 3, 4, 1), (1, 1, 2, 4)),
    "key": ("keyval", 0, 4, (1, 2, 4, 3), (1, 2, 4, 4)),
    "keyb": ("keyval", 4, 8, (1, 2, 3, 4), (1, 1, 2, 2)),
}
INDEX = {name: index for index, name in enumerate(PARTS)}
LAG = 2


SCHEDULE = {
    "middle": (
        ("gate2", 0, 0),
        ("gate2", 0, 1),
        ("gate2", 0, 2),
    ),
    "attend0": (
        ("gate2", 0, 3),
        ("gate2", 0, 4),
    ),
    "attend1": (
        ("gate2", 0, 5),
    ),
    "attend2": (
        ("gate2", 0, 6),
        ("gate2", 0, 7),
    ),
    "attend3": (
        ("gate2", 0, 8),
    ),
    "back": (
        ("gate2", 1, 0),
        ("gate2", 1, 2),
    ),
    "first": (
        ("gate2", 2, 2),
        ("gate", 1, 0),
        ("gate2", 2, 4),
        ("up2", 0, 1),
        ("up2", 0, 2),
        ("up2", 0, 3),
        ("up2", 0, 4),
        ("up2", 0, 5),
        ("up2", 0, 6),
    ),
    "query": (
        ("gate2", 1, 4),
        ("gate2", 1, 6),
        ("gate", 0, 0),
        ("up", 0, 0),
        ("down", 0, 0),
        ("up", 0, 2),
    ),
    "keyb": (
        ("gate2", 2, 0),
        ("up2", 0, 0),
    ),
    "gain0": (
        ("gate2", 2, 6),
        ("down", 1, 0),
        ("gate2", 0, 9),
        ("rest", 0, 0),
        ("down", 0, 1),
        ("down", 0, 2),
        ("out", 0, 0),
        ("out", 0, 1),
        ("out", 0, 2),
        ("out", 0, 3),
        ("key", 0, 0),
        ("up2", 1, 0),
        ("gate2", 3, 0),
        ("gate2", 3, 2),
        ("query", 0, 0),
        ("gate2", 3, 4),
        ("up2", 1, 2),
        ("query", 0, 1),
        ("key", 0, 2),
        ("up2", 1, 4),
        ("up", 1, 0),
        ("gate", 2, 0),
        ("up2", 1, 6),
        ("query", 0, 2),
        ("gate2", 3, 6),
        ("keyb", 0, 0),
        ("query", 0, 3),
        ("keyb", 0, 1),
        ("down", 2, 0),
        ("gate2", 1, 8),
        ("query", 1, 0),
        ("keyb", 0, 2),
        ("up2", 2, 0),
        ("gate", 3, 0),
    ),
    "gain1": (
        ("rest", 1, 0),
        ("keyb", 0, 3),
        ("query", 1, 2),
        ("down", 1, 1),
        ("up2", 2, 4),
        ("down", 3, 0),
        ("key", 1, 0),
        ("gate2", 2, 8),
        ("down", 1, 2),
    ),
    "last": (
        ("rest", 2, 0),
        ("out", 1, 0),
        ("keyb", 1, 0),
        ("keyb", 1, 2),
        ("out", 1, 2),
        ("query", 2, 0),
        ("down", 2, 1),
        ("gate2", 3, 8),
        ("down", 2, 2),
        ("up", 2, 0),
        ("up2", 3, 0),
        ("up2", 3, 4),
        ("out", 2, 0),
        ("key", 2, 0),
        ("keyb", 2, 0),
        ("query", 3, 0),
        ("rest", 3, 0),
        ("keyb", 2, 2),
        ("out", 2, 2),
        ("up", 3, 0),
        ("down", 3, 1),
        ("down", 3, 2),
        ("key", 3, 0),
        ("out", 3, 0),
        ("keyb", 3, 0),
        ("keyb", 3, 2),
        ("out", 3, 2),
    ),
}


def round_up(value, unit):
    return -(-value // unit) * unit


def length(name):
    return PARTS[name][2] - PARTS[name][1]


def step_span(name, level):
    return PARTS[name][4][level]


def step_layout(bits):
    places, total = {}, 0
    for name in PARTS:
        for level in range(bits):
            places[name, level] = total
            total += -(-length(name) // step_span(name, level))
    return places, total


def stage_copies(bits):
    return 1 + (1 << min(bits, 2)) - 1 + (1 << max(bits - 2, 0)) - 1


def bit_of(number, bit):
    return (number // (1 << bit)) % 2


def flip(number, bit):
    return number + (1 << bit) * (1 - 2 * bit_of(number, bit))


def dot(left, right):
    return jnp.dot(left, right, preferred_element_type=F32)


def dot_rows(left, right):
    return lax.dot_general(left, right, (((1,), (1,)), ((), ())), preferred_element_type=F32)


def dot_cols(left, right):
    return lax.dot_general(left, right, (((0,), (0,)), ((), ())), preferred_element_type=F32)


def at_chunk(index, size=CHUNK):
    return pl.ds(index * size, size)


def loop(first, last, body, **options):
    def step(at, carry):
        body(at)
        return carry

    lax.fori_loop(first, last, step, 0, **options)


def layer_kernel(sizes, in_names, out_names, scratch_names, *refs):
    micro, block, width, hidden_width, devices, groups = sizes
    r = dict(zip(in_names + out_names + scratch_names, refs))
    lower = devices // groups
    bits = groups.bit_length() - 2
    count = 1 << bits
    half = count // 2
    step_places, _ = step_layout(bits)
    orders = {name: [bit for bit in part[3] if bit <= bits] for name, part in PARTS.items()}
    rows_all = micro * block
    chunks = width // CHUNK
    full = hidden_width // CHUNK
    tail = hidden_width % CHUNK
    depth = r["ring_gate"].shape[0]
    kept = full - depth
    scale = 1.0 / math.sqrt(HEAD)

    schedule = SCHEDULE
    if bits != 4:
        schedule = {"last": [
            (name, level, first)
            for level in range(bits) for name in PARTS
            for first in range(0, length(name), step_span(name, min(level + 1, bits - 1)))
        ]}

    position = lax.axis_index("seq")
    me, rest = position // lower, position % lower
    core = me % 2
    my_unit = me // 2
    after = ((position + 1) % devices,)
    behind = ((position + devices - 1) % devices,)

    def partner(*some):
        other = me
        for bit in some:
            other = flip(other, bit)
        return (other * lower + rest,)

    stages = [[0], list(range(1, bits + 1))[:2], list(range(1, bits + 1))[2:]]
    stages = [stage for stage in stages if stage]
    peers = [
        [partner(*[bit for place, bit in enumerate(stage) if mask >> place & 1]) for mask in range(1, 1 << len(stage))]
        for stage in stages
    ]


    def local_copy(source, target, index):
        return pltpu.make_async_copy(source, target, r["local_sem"].at[index])

    def remote_copy(source, target, sems, index, device):
        send, recv = r[sems + "_send"], r[sems + "_recv"]
        return pltpu.make_async_remote_copy(
            src_ref=source, dst_ref=target, send_sem=send.at[index], recv_sem=recv.at[index],
            device_id=device, device_id_type=MESH,
        )

    load_tokens = local_copy(r["tokens"], r["x"], 0)
    load_cot = local_copy(r["cotangent"], r["col_cot"].at[0], 1)
    load_out = local_copy(r["w_out"], r["wo"], 2)
    rings = ("ring_gate", "ring_up", "ring_down")
    past = pl.ds(full * CHUNK, tail)
    load_tails = [
        local_copy(r[name].at[past, :], r["tail_" + name[2:]], 3 + index)
        for index, name in enumerate(("w_gate", "w_up", "w_down"))
    ]
    attention_weights = [
        pltpu.make_async_copy(r[name].at[at_chunk(slot), :], r[ring].at[slot], r["ring_sem"].at[index, slot])
        for index, (name, ring) in enumerate(zip(("w_query", "w_key", "w_value"), rings))
        for slot in range(depth)
    ]

    def hidden_weights(chunk, place):
        slot = place % depth
        return [
            pltpu.make_async_copy(r[name].at[at_chunk(chunk), :], r[ring].at[slot], r["ring_sem"].at[index, slot])
            for index, (name, ring) in enumerate(zip(("w_gate", "w_up", "w_down"), rings))
        ]

    def pair_copies():
        plan = {}
        for name in ROWS:
            plan[name] = (r["row_" + name].at[:, 1 - core], r["peer_" + name])
        plan["cot"] = (r["cotangent"], r["col_cot"].at[1])
        for name in ("branch", "dquery", "dkeyval", "dkvback"):
            plan[name] = (r["col_" + name].at[0], r["col_" + name].at[1])
        return {
            name: remote_copy(source, target, "pair", index, partner(0))
            for index, (name, (source, target)) in enumerate(plan.items())
        }

    pair = pair_copies()
    ready = set()

    def need(name):
        if name not in ready and name not in CHUNKED:
            ready.add(name)
            pair[name].wait_recv()

    def pair_chunk(first, last=None):
        ref = r["col_hidden"]
        some = pl.ds(first, 1 if last is None else last - first)
        return pltpu.make_async_remote_copy(
            src_ref=ref.at[0, some], dst_ref=ref.at[1, some],
            send_sem=r["chunk_send"].at[0], recv_sem=r["chunk_recv"].at[first],
            device_id=partner(0), device_id_type=MESH,
        )

    halo_out = remote_copy(r["x"], r["x_before"], "halo", 0, after)
    halo_back = remote_copy(r["back_out"], r["back_in"], "halo", 1, behind)

    load_tokens.start()
    r["x_before"][...] = jnp.zeros_like(r["x_before"])
    barrier = pltpu.get_barrier_semaphore()
    greeted = [after, behind] + [device for stage in peers for device in stage]
    for device in greeted:
        pl.semaphore_signal(barrier, inc=1, device_id=device, device_id_type=MESH)
    for copy in attention_weights:
        copy.start()
    for part in range(2):
        r["col_hidden"][0, full, part] = jnp.zeros((rows_all, CHUNK), BF16)


    def unit_at(order, slot):
        unit = my_unit
        for place, bit in enumerate(order):
            rel = (slot // (1 << (bits - 1 - place))) % 2
            unit = unit + (1 << (bit - 1)) * rel * (1 - 2 * bit_of(me, bit))
        return unit

    def factors(name, base):
        matrix = PARTS[name][0]
        units = [unit_at(orders[name], base + slot) for slot in range(half)]
        pairs = []
        for row, col in MATRICES[matrix]:
            need(row)
            need(col)
            for source in range(2):
                parts = [
                    r["row_" + row][unit, core] if source == 0 else r["peer_" + row][unit] for unit in units
                ]
                pairs.append((jnp.concatenate(parts, axis=0), col, source))
        return pairs

    def product(pairs, chunk):
        total = None
        for left, col, source in pairs:
            if col in CHUNKED:
                right = r["col_hidden"][source, chunk, CHUNKED.index(col)]
            else:
                right = r["col_" + col][source, :, at_chunk(chunk)]
            term = dot(left, right)
            total = term if total is None else total + term
        return total.reshape(half, total.shape[0] // half, CHUNK)

    def step_copy(name, level, first, last):
        size = half >> level
        some = pl.ds(first, last - first)
        if level == 0:
            source = r["send_" + name].at[some]
        else:
            source = r[f"land_{name}{level - 1}"].at[some, pl.ds(size, size)]
        place = step_places[name, level] + first // step_span(name, level)
        return pltpu.make_async_remote_copy(
            src_ref=source, dst_ref=r[f"land_{name}{level}"].at[some],
            send_sem=r["step_send"].at[INDEX[name], level], recv_sem=r["step_recv"].at[place],
            device_id=partner(orders[name][level]), device_id_type=MESH,
        )

    def send_products(name):
        pairs = factors(name, half)
        for at in range(length(name)):
            r["send_" + name][at] = product(pairs, PARTS[name][1] + at).astype(BF16)
            step_copy(name, 0, at, at + 1).start()

    def arrive(name, level, first):
        last = min(first + step_span(name, min(level + 1, bits - 1)), length(name))
        matrix, base = PARTS[name][:2]
        here = r[f"land_{name}{level}"]
        pairs = factors(name, 0) if level == 0 else None
        size = half >> level
        span = step_span(name, level)
        for at in range(first, last, span):
            step_copy(name, level, at, min(at + span, last)).wait_recv()
        for at in range(first, last):
            if level == 0:
                own = product(pairs, base + at)
            else:
                own = r[f"land_{name}{level - 1}"][at, :size].astype(F32)
            total = own + here[at].astype(F32)
            if level < bits - 1:
                here[at] = total.astype(BF16)
            elif matrix in ("gate", "up"):
                rows = total.shape[1]
                for part in range(CHUNK // 128):
                    place = ((base + at) * (CHUNK // 128) + part) * rows
                    r["turn_" + matrix][pl.ds(place, rows), :] = total[0, :, 128 * part : 128 * (part + 1)]
            else:
                r["total_" + name][at] = total[0]
        if level < bits - 1:
            step_copy(name, level + 1, first, last).start()
        else:
            unfinished[matrix] -= last - first
            if not unfinished[matrix]:
                finish(matrix)

    unfinished = {}
    for name, part in PARTS.items():
        unfinished[part[0]] = unfinished.get(part[0], 0) + length(name)

    def finish(matrix):
        if matrix in ("gate", "up"):
            flat, turn = r["flat_" + matrix], r["turn_" + matrix]
            whole = hidden_width // 128
            steps = hidden_width // 64
            rows = turn.shape[0] // (whole + 1)
            few = rows // 2
            even = [turn[pl.ds(rows * j, few, stride=2), :] for j in range(whole + 1)]
            odd = [pltpu.roll(turn[pl.ds(rows * j + 1, few, stride=2), :], 64, 1) for j in range(whole + 1)]
            low = lax.broadcasted_iota(jnp.int32, (few, 128), 1) < 64
            for j in range(whole):
                flat[pl.ds(j, few, stride=steps), :] = even[j]
                flat[pl.ds(whole + 1 + j, few, stride=steps), :] = jnp.where(low, odd[j], odd[j + 1])
            flat[pl.ds(whole, few, stride=steps), :] = jnp.where(low, even[whole], odd[0])
            return
        per_row = width // 128
        for name, part in PARTS.items():
            if part[0] != matrix:
                continue
            for at in range(length(name)):
                total = r["total_" + name][at]
                for piece in range(CHUNK // 128):
                    column = (part[1] + at) * (CHUNK // 128) + piece
                    target = "flat_value" if column >= per_row else "flat_" + matrix
                    rows = r[target].shape[0] // per_row
                    r[target][pl.ds(column % per_row, rows, stride=per_row), :] = total[:rows, 128 * piece : 128 * (piece + 1)]

    def gain_copy(stage, index):
        base = sum(len(group) + 1 for group in peers[:stage])
        return remote_copy(
            r["gain_buf"].at[base], r["gain_buf"].at[base + 1 + index], "gain", base - stage + index, peers[stage][index]
        )

    def gain_start(stage, value):
        r["gain_buf"][sum(len(group) + 1 for group in peers[:stage])] = value
        for index in range(len(peers[stage])):
            gain_copy(stage, index).start()

    def gain_step(stage):
        base = sum(len(group) + 1 for group in peers[:stage])
        total = r["gain_buf"][base]
        for index in range(len(peers[stage])):
            gain_copy(stage, index).wait_recv()
            total = total + r["gain_buf"][base + 1 + index]
        if stage + 1 < len(peers):
            gain_start(stage + 1, total)
            return
        for row, name in enumerate(("gain_attn_sum", "gain_mlp_sum")):
            for j in range(width // 128):
                r[name][j : j + 1, :] = total[row : row + 1, 128 * j : 128 * (j + 1)]

    def arrivals(point):
        for name, level, first in schedule.get(point, ()):
            arrive(name, level, first)


    def some_rows(at):
        return pl.ds(at * block, block)

    def row_scale(value):
        return lax.rsqrt(jnp.mean(value * value, axis=-1, keepdims=True) + EPSILON)

    def first_norm(source, target):
        def body(at):
            value = source[some_rows(at), :].astype(F32)
            target[some_rows(at), :] = (value * row_scale(value) * r["gain_attn"][...]).astype(BF16)

        loop(0, micro, body)

    def by_owner(name, source):
        ref = r["row_" + name]
        ref[...] = source[...].T.reshape(ref.shape)
        pair[name].start()

    def project(left, ring, target):
        target[...] = dot(left[...], r[ring][...].reshape(width, width)).astype(BF16)

    act, other = r["act"], r["other"]
    load_tokens.wait()
    pl.semaphore_wait(barrier, len(greeted))
    pl.when(position < devices - 1)(halo_out.start)
    first_norm(r["x"], act)
    load_out.start()
    load_cot.start()
    for copy in load_tails:
        copy.start()
    for index, (ring, target) in enumerate(zip(rings, ("queries", "keys", "values"))):
        for copy in attention_weights[index * depth : (index + 1) * depth]:
            copy.wait()
        project(act, ring, r[target])
    by_owner("first", act)
    pl.when(position > 0)(halo_out.wait_recv)
    first_norm(r["x_before"], other)
    project(other, "ring_up", r["keys_before"])
    project(other, "ring_down", r["values_before"])
    for slot in range(depth):
        for copy in hidden_weights(slot, slot):
            copy.start()

    quad = CHUNK // HEAD
    start = position * block
    lane_head = lax.broadcasted_iota(jnp.int32, (block, CHUNK), 1) // HEAD
    key_at = start - WIN + lax.broadcasted_iota(jnp.int32, (2 * block, CHUNK), 0)
    query_at = start + lax.broadcasted_iota(jnp.int32, (1, CHUNK), 1) % block

    def stacked(value):
        return jnp.concatenate([jnp.where(lane_head == h, value, jnp.zeros_like(value)) for h in range(quad)], axis=0)

    def unstacked(value):
        total = jnp.zeros((block, CHUNK), F32)
        for h in range(quad):
            total = jnp.where(lane_head == h, value[h * block : (h + 1) * block], total)
        return total

    def unit(index):
        return index // chunks, some_rows(index // chunks), at_chunk(index % chunks)

    def both(before, own, rows, lanes):
        return jnp.concatenate([r[before][rows, lanes], r[own][rows, lanes]], axis=0)

    def allowed(which):
        def body(at, carry):
            end, low = carry
            end = end + r["lengths"][which, at]
            return end, jnp.where(query_at >= end, end, low)

        _, low = lax.fori_loop(
            0, r["lengths"].shape[1], body, (jnp.int32(0), jnp.zeros((1, CHUNK), jnp.int32))
        )
        low = jnp.maximum(low, query_at - (WIN - 1))
        return (key_at >= low) & (key_at <= query_at)

    def scores(which, keys, queries):
        return jnp.where(allowed(which), dot_rows(keys, queries) * scale, -1e30)

    def attend(index):
        which, rows, lanes = unit(index)
        logits = scores(which, both("keys_before", "keys", rows, lanes), stacked(r["queries"][rows, lanes]))
        peak = jnp.max(logits, axis=0, keepdims=True)
        powers = jnp.exp(logits - peak)
        total = jnp.sum(powers, axis=0, keepdims=True)
        r["log_sums"][index] = jnp.broadcast_to(peak + jnp.log(total), (8, CHUNK))
        probability = (powers / total).astype(BF16)
        mixed = dot_cols(probability, both("values_before", "values", rows, lanes))
        act[rows, lanes] = unstacked(mixed).astype(BF16)

    pair["cot"].start()
    loop(0, micro * chunks, attend, unroll=2)
    load_out.wait()
    middle = r["input_grad"]

    middle[...] = r["x"][...].astype(F32) + dot(act[...], r["wo"][...])

    def second_norm(at):
        value = middle[some_rows(at), :]
        other[some_rows(at), :] = (value * row_scale(value) * r["gain_mlp"][...]).astype(BF16)

    loop(0, micro, second_norm)
    by_owner("second", other)


    def hidden_part(gate, up, grad_hidden):
        sigmoid = jax.nn.sigmoid(gate)
        silu = gate * sigmoid
        hidden = (silu * up).astype(BF16)
        dgate = (grad_hidden * up * sigmoid * (1.0 + gate * (1.0 - sigmoid))).astype(BF16)
        return hidden, dgate, (grad_hidden * silu).astype(BF16)

    columns = r["columns"]

    def hidden_chunk(at, prefetch):
        slot = at % depth
        for copy in hidden_weights(at, at):
            copy.wait()
        wait_chunk(at - LAG)
        hidden, dgate, dup = hidden_part(
            dot_rows(other[...], r["ring_gate"][slot]),
            dot_rows(other[...], r["ring_up"][slot]),
            dot_rows(r["col_cot"][0], r["ring_down"][slot]),
        )
        lanes = at_chunk(at)
        form_chunk(at - LAG)
        r["hidden"][:, lanes] = hidden
        r["col_hidden"][0, at, 0] = dgate
        r["col_hidden"][0, at, 1] = dup
        columns[lanes, :] = hidden.astype(F32).T
        pair_chunk(at).start()
        send_chunk(at - LAG)
        if prefetch:
            for copy in hidden_weights(at + depth, at + depth):
                copy.start()

    early_factors = {}

    def early(at):
        return [
            (name, at - part[1]) for name, part in PARTS.items() if part[0] in ("gate", "up") and part[1] <= at < part[2]
        ]

    def wait_chunk(at):
        if at >= 0:
            pair_chunk(at).wait_recv()

    def form_chunk(at):
        for name, place in early(at):
            if name not in early_factors:
                early_factors[name] = factors(name, half)
            r["send_" + name][place] = product(early_factors[name], at).astype(BF16)

    def send_chunk(at):
        for name, place in early(at):
            step_copy(name, 0, place, place + 1).start()

    load_cot.wait()
    for copy in load_tails:
        copy.wait()
    for at in range(full):
        hidden_chunk(at, at < kept)
    hidden, dgate, dup = hidden_part(
        dot_rows(other[...], r["tail_gate"][...]),
        dot_rows(other[...], r["tail_up"][...]),
        dot_rows(r["col_cot"][0], r["tail_down"][...]),
    )
    r["hidden"][:, past] = hidden
    r["col_hidden"][0, full, 0, :, :tail] = dgate
    r["col_hidden"][0, full, 1, :, :tail] = dup
    pair_chunk(full).start()
    r["square"][...] = jnp.zeros_like(r["square"])
    r["square"][:, :tail] = hidden.astype(F32)
    columns[pl.ds(full * CHUNK, CHUNK), :] = r["square"][...].T
    own_rows = hidden_width // groups
    held_rows = r["row_hidden"].shape[2]
    for owner in range(groups):
        r["row_hidden"][owner // 2, owner % 2] = columns[pl.ds(owner * own_rows, held_rows), :].astype(BF16)
    pair["hidden"].start()
    for at in range(full - LAG, full + 1):
        wait_chunk(at)
        form_chunk(at)
        send_chunk(at)
    for name, part in PARTS.items():
        if part[0] == "down":
            send_products(name)


    sums = [pl.ds(n * CHUNK, CHUNK) for n in range(2 * chunks)]

    def fold(*pieces):
        back = None
        for dgate, dup, gate_ref, up_ref in pieces:
            one = dot(dgate, gate_ref[...]) + dot(dup, up_ref[...])
            back = one if back is None else back + one
        for n in range(chunks):
            columns[sums[n], :] += back[:, n * CHUNK : (n + 1) * CHUNK]

    def fold_chunks(places):
        pieces = []
        for at in places:
            chunk = at - depth if at < full + depth else at - depth - full
            if at >= full + depth:
                for copy in hidden_weights(chunk, at)[:2]:
                    copy.wait()
            pieces.append((
                r["col_hidden"][0, chunk, 0], r["col_hidden"][0, chunk, 1],
                *(r[ring].at[at % depth] for ring in rings[:2]),
            ))
        fold(*pieces)
        for at in places:
            if at < full + kept:
                for copy in hidden_weights(at - full, at + depth)[:2]:
                    copy.start()

    for some in sums[:chunks]:
        columns[some, :] = jnp.zeros((CHUNK, CHUNK), F32)
    fold((
        r["col_hidden"][0, full, 0, :, :tail], r["col_hidden"][0, full, 1, :, :tail], r["tail_gate"], r["tail_up"],
    ))
    for at in range(full, 2 * full, 2):
        fold_chunks(range(at, min(at + 2, 2 * full)))
    for copy in attention_weights:
        copy.start()

    def output_load(chunk):
        return hidden_weights(chunk, chunk)[2]

    def output_chunks(first, last):
        for chunk in range(first, last):
            output_load(chunk).wait()
        total = None
        for chunk in range(first, last):
            term = dot(r["hidden"][:, at_chunk(chunk)], r["ring_down"][chunk % depth])
            total = term if total is None else total + term
        for n in range(chunks):
            columns[sums[chunks + n], :] += total[:, n * CHUNK : (n + 1) * CHUNK]
        for chunk in range(first + depth, min(last + depth, full)):
            output_load(chunk).start()

    def form_output():
        rest = dot(r["hidden"][:, past], r["tail_down"][...])
        for n in range(chunks):
            columns[sums[chunks + n], :] += rest[:, n * CHUNK : (n + 1) * CHUNK]
        for first in range(0, full, 2):
            output_chunks(first, min(first + 2, full))
        for n in range(chunks):
            r["output"][:, at_chunk(n)] = columns[sums[chunks + n], :].astype(BF16)

    def summed(at, base):
        return jnp.concatenate(
            [columns[pl.ds((base + n) * CHUNK + at * block, block), :] for n in range(chunks)],
            axis=1,
        )

    def norm_backward(grad, value, gain):
        inverse = row_scale(value)
        normed = value * inverse
        scaled = grad * gain
        mean = jnp.mean(scaled * normed, axis=-1, keepdims=True)
        return inverse * (scaled - normed * mean), jnp.sum(grad * normed, axis=0, keepdims=True)

    def middle_backward(at, gain_sum):
        rows = some_rows(at)
        value = middle[rows, :]
        for n in range(chunks):
            place = pl.ds((chunks + n) * CHUNK + at * block, block)
            columns[place, :] = value[:, n * CHUNK : (n + 1) * CHUNK]
        grad, part = norm_backward(summed(at, 0), value, r["gain_mlp"][...])
        grad = grad + r["col_cot"][0, rows, :].astype(F32)
        middle[rows, :] = grad
        r["col_branch"][0, rows, :] = grad.astype(BF16)
        return gain_sum + part

    gain_mlp_sum = lax.fori_loop(0, micro, middle_backward, jnp.zeros((1, width), F32))
    pair["branch"].start()
    by_owner("attended", act)
    first_norm(r["x_before"], r["back_out"])
    by_owner("before", r["back_out"])

    r["grad_attended"][...] = dot_rows(r["col_branch"][0], r["wo"][...]).astype(BF16)


    def attend_backward(index):
        which, rows, lanes = unit(index)
        keys = both("keys_before", "keys", rows, lanes)
        values = both("values_before", "values", rows, lanes)
        queries = stacked(r["queries"][rows, lanes])
        grads = stacked(r["grad_attended"][rows, lanes])
        probability = jnp.exp(scores(which, keys, queries) - r["log_sums"][index][:1])
        grad_prob = dot_rows(values, grads)
        delta = jnp.sum(probability * grad_prob, axis=0, keepdims=True)
        grad_scores = (scale * probability * (grad_prob - delta)).astype(BF16)
        r["col_dquery"][0, rows, lanes] = unstacked(dot_cols(grad_scores, keys)).astype(BF16)
        dkey = dot(grad_scores, queries).astype(BF16)
        dvalue = dot(probability.astype(BF16), grads).astype(BF16)
        lanes_value = at_chunk(chunks + index % chunks)
        r["col_dkvback"][0, rows, lanes] = dkey[:block]
        r["col_dkvback"][0, rows, lanes_value] = dvalue[:block]
        r["col_dkeyval"][0, rows, lanes] = dkey[block:]
        r["col_dkeyval"][0, rows, lanes_value] = dvalue[block:]

    arrivals("middle")
    for at in range(micro):
        loop(at * chunks, (at + 1) * chunks, attend_backward, unroll=2)
        arrivals("attend" + str(at))
    for name in ("dquery", "dkeyval", "dkvback"):
        pair[name].start()
    def through_keys(ref, at):
        return dot_rows(ref[0, :, :width], r["ring_up"][at]) + dot_rows(ref[0, :, width:], r["ring_down"][at])

    def back_chunk(at):
        r["back_out"][:, at_chunk(at)] = through_keys(r["col_dkvback"], at).astype(BF16)

    def first_chunk(at):
        columns[at_chunk(at), :] = through_keys(r["col_dkeyval"], at) + dot_rows(
            r["col_dquery"][0], r["ring_gate"][at]
        )

    for copy in attention_weights:
        copy.wait()
    loop(0, chunks, back_chunk)
    pl.when(position > 0)(halo_back.start)
    arrivals("back")
    send_products("out")
    arrivals("out")

    def gain_parts(at, gain_sum):
        rows = some_rows(at)
        for grad, name in ((summed(at, 0), "x"), (r["back_out"][rows, :].astype(F32), "x_before")):
            value = r[name][rows, :].astype(F32)
            gain_sum = gain_sum + jnp.sum(grad * (value * row_scale(value)), axis=0, keepdims=True)
        return gain_sum

    for name in ("query", "key", "keyb"):
        send_products(name)
        arrivals(name)
    loop(0, chunks, first_chunk)
    gain_attn_sum = lax.fori_loop(0, micro, gain_parts, jnp.zeros((1, width), F32))
    gain_start(0, jnp.concatenate([gain_attn_sum, gain_mlp_sum, jnp.zeros((6, width), F32)], axis=0))
    arrivals("first")
    for chunk in range(depth):
        output_load(chunk).start()

    def input_backward(at):
        rows = some_rows(at)
        back = jnp.where(position < devices - 1, r["back_in"][rows, :].astype(F32), 0.0)
        grad, _ = norm_backward(summed(at, 0) + back, r["x"][rows, :].astype(F32), r["gain_attn"][...])
        middle[rows, :] = middle[rows, :] + grad

    for stage in range(len(peers)):
        if stage == 1:
            form_output()
        gain_step(stage)
        arrivals("gain" + str(stage))
    pl.when(position < devices - 1)(halo_back.wait_recv)
    loop(0, micro, input_backward)
    arrivals("last")

    pl.when(position < devices - 1)(halo_out.wait_send)
    pl.when(position > 0)(halo_back.wait_send)
    for copy in pair.values():
        copy.wait_send()
    for stage, group in enumerate(peers):
        for index in range(len(group)):
            gain_copy(stage, index).wait_send()
    pair_chunk(0, full + 1).wait_send()
    for name in PARTS:
        for level in range(bits):
            step_copy(name, level, 0, length(name)).wait_send()


def layer(tokens, gain_attn, gain_mlp, weights, cotangent, lengths, micro, devices, groups):
    rows_all, width = tokens.shape
    hidden_width = weights["w_gate"].shape[0]
    block = rows_all // micro
    bits = groups.bit_length() - 2
    count = 1 << bits
    half = count // 2
    chunks = width // CHUNK
    padded = round_up(hidden_width, CHUNK)
    tail = hidden_width % CHUNK
    depth = chunks
    unit_rows = {name: width // groups for name in ROWS}
    unit_rows["hidden"] = round_up(hidden_width // groups, 16)
    widths = {name: width for name in COLS}
    widths.update(dkeyval=2 * width, dkvback=2 * width)

    inputs = {"tokens": tokens, "cotangent": cotangent, **weights}
    any_spec = pl.BlockSpec(memory_space=pl.ANY)
    vmem_spec = pl.BlockSpec(memory_space=pltpu.VMEM)
    in_specs = [any_spec] * len(inputs) + [vmem_spec] * 2 + [pl.BlockSpec(memory_space=pltpu.SMEM)]
    inputs.update(gain_attn=gain_attn[None], gain_mlp=gain_mlp[None], lengths=lengths)

    outs = {
        "output": ((rows_all, width), BF16),
        "input_grad": ((rows_all, width), F32),
        "gain_attn_sum": ((width // 128, 128), F32),
        "gain_mlp_sum": ((width // 128, 128), F32),
    }
    own = {"query": width * width, "keyval": width * width, "value": width * width, "out": width * width}
    own.update(gate=width * hidden_width, up=width * hidden_width, down=width * hidden_width)
    for name, size in own.items():
        outs["flat_" + name] = ((size // groups // 128, 128), F32)

    scratch = {
        "x": pltpu.VMEM((rows_all, width), BF16),
        "x_before": pltpu.VMEM((rows_all, width), BF16),
        "act": pltpu.VMEM((rows_all, width), BF16),
        "other": pltpu.VMEM((rows_all, width), BF16),
        "queries": pltpu.VMEM((rows_all, width), BF16),
        "keys": pltpu.VMEM((rows_all, width), BF16),
        "values": pltpu.VMEM((rows_all, width), BF16),
        "keys_before": pltpu.VMEM((rows_all, width), BF16),
        "values_before": pltpu.VMEM((rows_all, width), BF16),
        "grad_attended": pltpu.VMEM((rows_all, width), BF16),
        "back_out": pltpu.VMEM((rows_all, width), BF16),
        "back_in": pltpu.VMEM((rows_all, width), BF16),
        "log_sums": pltpu.VMEM((micro * chunks, 8, CHUNK), F32),
        "wo": pltpu.VMEM((width, width), BF16),
        "ring_gate": pltpu.VMEM((depth, CHUNK, width), BF16),
        "ring_up": pltpu.VMEM((depth, CHUNK, width), BF16),
        "ring_down": pltpu.VMEM((depth, CHUNK, width), BF16),
        "tail_gate": pltpu.VMEM((tail, width), BF16),
        "tail_up": pltpu.VMEM((tail, width), BF16),
        "tail_down": pltpu.VMEM((tail, width), BF16),
        "hidden": pltpu.VMEM((rows_all, padded), BF16),
        "columns": pltpu.VMEM((padded, rows_all), F32),
        "square": pltpu.VMEM((rows_all, CHUNK), F32),
        "gain_buf": pltpu.VMEM((stage_copies(bits) + 3, 8, width), F32),
    }
    for name in ROWS:
        scratch["row_" + name] = pltpu.VMEM((count, 2, unit_rows[name], rows_all), BF16)
        scratch["peer_" + name] = pltpu.VMEM((count, unit_rows[name], rows_all), BF16)
    for name in COLS:
        if name not in CHUNKED:
            scratch["col_" + name] = pltpu.VMEM((2, rows_all, widths[name]), BF16)
    scratch["col_hidden"] = pltpu.VMEM((2, padded // CHUNK, len(CHUNKED), rows_all, CHUNK), BF16)
    for name, (matrix, first, last, _, _) in PARTS.items():
        rows = unit_rows[MATRICES[matrix][0][0]]
        scratch["send_" + name] = pltpu.VMEM((last - first, half, rows, CHUNK), BF16)
        for level in range(bits):
            scratch[f"land_{name}{level}"] = pltpu.VMEM((last - first, half >> level, rows, CHUNK), BF16)
        if matrix in ("gate", "up"):
            scratch["turn_" + matrix] = pltpu.VMEM((padded // 128 * rows, 128), F32)
        else:
            scratch["total_" + name] = pltpu.VMEM((last - first, rows, CHUNK), F32)
    sems = {"local_sem": (6,), "ring_sem": (3, depth)}
    sems.update(chunk_send=(1,), chunk_recv=(padded // CHUNK,))
    sems.update(step_send=(len(PARTS), bits), step_recv=(step_layout(bits)[1],))
    for name, number in (("pair", len(ROWS) + len(COLS) - len(CHUNKED)), ("halo", 2), ("gain", stage_copies(bits))):
        sems[name + "_send"] = sems[name + "_recv"] = (number,)
    for name, shape in sems.items():
        scratch[name] = pltpu.SemaphoreType.DMA(shape)

    sizes = (micro, block, width, hidden_width, devices, groups)
    results = pl.pallas_call(
        functools.partial(layer_kernel, sizes, tuple(inputs), tuple(outs), tuple(scratch)),
        out_shape=[jax.ShapeDtypeStruct(*spec) for spec in outs.values()],
        in_specs=in_specs,
        out_specs=[vmem_spec] * len(outs),
        scratch_shapes=list(scratch.values()),
        compiler_params=pltpu.CompilerParams(
            collective_id=0, has_side_effects=True, vmem_limit_bytes=63 * 2**20
        ),
        name="layer",
    )(*inputs.values())
    return dict(zip(outs, handed_on(results)))


def hand_on_kernel(count, *refs):
    sources, targets, passing = (refs[part * count : (part + 1) * count] for part in range(3))
    sems = refs[-1]
    arriving = [
        pltpu.make_async_copy(source, middle, sems.at[0, index])
        for index, (source, middle) in enumerate(zip(sources, passing))
    ]
    leaving = [
        pltpu.make_async_copy(middle, target, sems.at[1, index])
        for index, (middle, target) in enumerate(zip(passing, targets))
    ]
    for copy in arriving:
        copy.start()
    for before, copy in zip(arriving, leaving):
        before.wait()
        copy.start()
    for copy in leaving:
        copy.wait()


def handed_on(arrays):
    any_spec = pl.BlockSpec(memory_space=pl.ANY)
    count = len(arrays)
    return pl.pallas_call(
        functools.partial(hand_on_kernel, count),
        out_shape=[jax.ShapeDtypeStruct(array.shape, array.dtype) for array in arrays],
        in_specs=[any_spec] * count,
        out_specs=[any_spec] * count,
        scratch_shapes=[pltpu.VMEM(array.shape, array.dtype) for array in arrays]
        + [pltpu.SemaphoreType.DMA((2, count))],
        name="hand_on",
    )(*arrays)


def per_device(
    tokens, gain_attn, gain_mlp, w_query, w_key, w_value, w_out, w_gate, w_up, w_down, cotangent, lengths
):
    devices = lax.axis_size("seq")
    groups = min(devices, MOST_GROUPS)
    lower = devices // groups
    micro, block, width = tokens.shape
    weights = dict(
        w_query=w_query, w_key=w_key, w_value=w_value, w_out=w_out, w_gate=w_gate.T, w_up=w_up.T, w_down=w_down
    )
    result = layer(
        tokens.reshape(micro * block, width), gain_attn, gain_mlp, weights,
        cotangent.reshape(micro * block, width), lengths, micro, devices, groups,
    )
    near = [[high * lower + low for low in range(lower)] for high in range(groups)]

    def slice_of(name):
        flat = result["flat_" + name].reshape(-1)
        if lower == 1:
            return flat
        return lax.psum_scatter(flat, "seq", axis_index_groups=near, tiled=True)

    gain_sums = [result["gain_attn_sum"].reshape(-1), result["gain_mlp_sum"].reshape(-1)]
    if lower > 1:
        gain_sums = lax.psum(gain_sums, "seq", axis_index_groups=near)
    return (
        result["output"].reshape(tokens.shape),
        result["input_grad"].reshape(tokens.shape),
        gain_sums[0],
        gain_sums[1],
        slice_of("query"),
        slice_of("keyval"),
        slice_of("value"),
        slice_of("out"),
        slice_of("gate"),
        slice_of("up"),
        slice_of("down"),
    )


def solution(mesh):
    tokens_spec = P(None, "seq", None)
    return jax.shard_map(
        per_device,
        mesh=mesh,
        in_specs=(tokens_spec,) + (P(),) * 9 + (tokens_spec, P()),
        out_specs=(tokens_spec, tokens_spec, P(), P()) + (P("seq"),) * 7,
        check_vma=False,
    )
```

profile of v0, /device:TPU:0, one launch (start us, length us, event | category | flops | bytes accessed | tf_op | source)
XLA Modules:
  0.0 145.7 jit_solution(8327015143015712070)
XLA Ops:
  0.6 141.8 %layer.1 = (bf16[256,1024]{1,0:T(8,128)(2,1)}, f32[256,1024]{1,0:T(8,128)}, f32[8,128]{1,0:T(8,128)}, f32[8,128]{1,0:T(8,128)}, f32[256,128]{1,0:T(8,128)}, /*in...) custom-call(bf16[256,1024]{1,0:T(8,128)(2,1)} %bitcast.19, ...), custom_call_target="tpu_custom_call" | custom-call | tf_op jit(solution)/shard_map/layer/pallas_call | solution.py:951
  142.5 3.1 %hand_on.1 = (bf16[256,1024]{1,0:T(8,128)(2,1)}, f32[256,1024]{1,0:T(8,128)}, f32[8,128]{1,0:T(8,128)}, f32[8,128]{1,0:T(8,128)}, f32[256,128]{1,0:T(8,128)}, /*...) custom-call(bf16[256,1024]{1,0:T(8,128)(2,1)} %get-tuple-element.33., ...), custom_call_target="tpu_custom_call" | custom-call | tf_op jit(solution)/shard_map/hand_on/pallas_call | solution.py:988
where the time goes:
time: 146 us
  Pallas kernels  145 us (99%)
    pallas_call x1, Pallas kernels, layer(): pl.pallas_call(functools.partial(layer_kernel, sizes, tuple(inputs), tupl...  142 us
    pallas_call x1, Pallas kernels, handed_on(): pl.pallas_call(functools.partial(hand_on_kernel, count), out_shape=[jax.S...  3.08 us

commit v1 on v0

--- a/solution.py
+++ b/solution.py
@@ -46,126 +46,128 @@
 
 SCHEDULE = {
     "middle": (
-        ("gate2", 0, 0),
-        ("gate2", 0, 1),
-        ("gate2", 0, 2),
+        (1, 0, 0),
+        (1, 0, 1),
+        (1, 0, 2),
+        (1, 0, 3),
+        (1, 0, 4),
     ),
     "attend0": (
-        ("gate2", 0, 3),
-        ("gate2", 0, 4),
+        (1, 0, 5),
     ),
     "attend1": (
-        ("gate2", 0, 5),
+        (1, 0, 6),
     ),
     "attend2": (
-        ("gate2", 0, 6),
-        ("gate2", 0, 7),
+        (1, 0, 7),
     ),
     "attend3": (
-        ("gate2", 0, 8),
+        (1, 0, 8),
+        (0, 0, 0),
+        (1, 1, 0),
+        (4, 0, 0),
+        (2, 0, 0),
+        (1, 0, 9),
+        (1, 1, 2),
     ),
     "back": (
-        ("gate2", 1, 0),
-        ("gate2", 1, 2),
+        (2, 0, 2),
     ),
     "first": (
-        ("gate2", 2, 2),
-        ("gate", 1, 0),
-        ("gate2", 2, 4),
-        ("up2", 0, 1),
-        ("up2", 0, 2),
-        ("up2", 0, 3),
-        ("up2", 0, 4),
-        ("up2", 0, 5),
-        ("up2", 0, 6),
+        (3, 0, 3),
+        (3, 0, 4),
+        (3, 0, 5),
+        (3, 0, 6),
+        (1, 2, 2),
+        (4, 1, 0),
+        (5, 0, 0),
     ),
     "query": (
-        ("gate2", 1, 4),
-        ("gate2", 1, 6),
-        ("gate", 0, 0),
-        ("up", 0, 0),
-        ("down", 0, 0),
-        ("up", 0, 2),
+        (1, 1, 4),
+        (1, 1, 6),
+        (4, 0, 1),
+        (1, 1, 8),
+        (0, 1, 0),
+        (3, 0, 0),
+    ),
+    "key": (
+        (1, 2, 0),
+        (3, 0, 1),
     ),
     "keyb": (
-        ("gate2", 2, 0),
-        ("up2", 0, 0),
+        (3, 0, 2),
     ),
     "gain0": (
-        ("gate2", 2, 6),
-        ("down", 1, 0),
-        ("gate2", 0, 9),
-        ("rest", 0, 0),
-        ("down", 0, 1),
-        ("down", 0, 2),
-        ("out", 0, 0),
-        ("out", 0, 1),
-        ("out", 0, 2),
-        ("out", 0, 3),
-        ("key", 0, 0),
-        ("up2", 1, 0),
-        ("gate2", 3, 0),
-        ("gate2", 3, 2),
-        ("query", 0, 0),
-        ("gate2", 3, 4),
-        ("up2", 1, 2),
-        ("query", 0, 1),
-        ("key", 0, 2),
-        ("up2", 1, 4),
-        ("up", 1, 0),
-        ("gate", 2, 0),
-        ("up2", 1, 6),
-        ("query", 0, 2),
-        ("gate2", 3, 6),
-        ("keyb", 0, 0),
-        ("query", 0, 3),
-        ("keyb", 0, 1),
-        ("down", 2, 0),
-        ("gate2", 1, 8),
-        ("query", 1, 0),
-        ("keyb", 0, 2),
-        ("up2", 2, 0),
-        ("gate", 3, 0),
+        (4, 0, 2),
+        (6, 0, 0),
+        (6, 0, 1),
+        (6, 0, 2),
+        (4, 1, 1),
+        (1, 3, 0),
+        (3, 1, 0),
+        (2, 1, 0),
+        (6, 0, 3),
+        (3, 1, 2),
+        (1, 2, 4),
+        (7, 0, 0),
+        (8, 0, 0),
+        (3, 1, 4),
+        (1, 2, 6),
+        (7, 0, 1),
+        (3, 1, 6),
+        (1, 3, 2),
+        (1, 2, 8),
+        (7, 0, 2),
+        (8, 0, 2),
+        (0, 2, 0),
+        (7, 0, 3),
+        (1, 3, 4),
+        (9, 0, 0),
+        (4, 2, 0),
+        (1, 3, 6),
+        (9, 0, 1),
+        (3, 2, 0),
+        (7, 1, 0),
+        (5, 1, 0),
+        (9, 0, 2),
     ),
     "gain1": (
-        ("rest", 1, 0),
-        ("keyb", 0, 3),
-        ("query", 1, 2),
-        ("down", 1, 1),
-        ("up2", 2, 4),
-        ("down", 3, 0),
-        ("key", 1, 0),
-        ("gate2", 2, 8),
-        ("down", 1, 2),
+        (4, 2, 1),
+        (9, 0, 3),
+        (7, 1, 2),
+        (3, 2, 4),
+        (0, 3, 0),
+        (4, 1, 2),
+        (8, 1, 0),
+        (1, 3, 8),
+        (4, 3, 0),
+        (5, 2, 0),
+        (6, 1, 0),
+        (9, 1, 0),
     ),
     "last": (
-        ("rest", 2, 0),
-        ("out", 1, 0),
-        ("keyb", 1, 0),
-        ("keyb", 1, 2),
-        ("out", 1, 2),
-        ("query", 2, 0),
-        ("down", 2, 1),
-        ("gate2", 3, 8),
-        ("down", 2, 2),
-        ("up", 2, 0),
-        ("up2", 3, 0),
-        ("up2", 3, 4),
-        ("out", 2, 0),
-        ("key", 2, 0),
-        ("keyb", 2, 0),
-        ("query", 3, 0),
-        ("rest", 3, 0),
-        ("keyb", 2, 2),
-        ("out", 2, 2),
-        ("up", 3, 0),
-        ("down", 3, 1),
-        ("down", 3, 2),
-        ("key", 3, 0),
-        ("out", 3, 0),
-        ("keyb", 3, 0),
-        ("keyb", 3, 2),
-        ("out", 3, 2),
+        (9, 1, 2),
+        (2, 2, 0),
+        (4, 3, 1),
+        (6, 1, 2),
+        (4, 2, 2),
+        (3, 3, 0),
+        (7, 2, 0),
+        (3, 3, 4),
+        (6, 2, 0),
+        (9, 2, 0),
+        (8, 2, 0),
+        (9, 2, 2),
+        (2, 3, 0),
+        (6, 2, 2),
+        (5, 3, 0),
+        (7, 3, 0),
+        (4, 3, 2),
+        (6, 3, 0),
+        (9, 3, 0),
+        (8, 3, 0),
+        (9, 3, 2),
+        (6, 3, 2),
     ),
 }
 
@@ -247,7 +249,7 @@
     schedule = SCHEDULE
     if bits != 4:
         schedule = {"last": [
-            (name, level, first)
+            (INDEX[name], level, first)
             for level in range(bits) for name in PARTS
             for first in range(0, length(name), step_span(name, min(level + 1, bits - 1)))
         ]}
@@ -488,8 +490,8 @@
                 r[name][j : j + 1, :] = total[row : row + 1, 128 * j : 128 * (j + 1)]
 
     def arrivals(point):
-        for name, level, first in schedule.get(point, ()):
-            arrive(name, level, first)
+        for part, level, first in schedule.get(point, ()):
+            arrive(tuple(PARTS)[part], level, first)
 
 
     def some_rows(at):
@@ -962,24 +964,30 @@
     return dict(zip(outs, handed_on(results)))
 
 
+PIECES = 4
+
+
 def hand_on_kernel(count, *refs):
     sources, targets, passing = (refs[part * count : (part + 1) * count] for part in range(3))
     sems = refs[-1]
-    arriving = [
-        pltpu.make_async_copy(source, middle, sems.at[0, index])
-        for index, (source, middle) in enumerate(zip(sources, passing))
-    ]
-    leaving = [
-        pltpu.make_async_copy(middle, target, sems.at[1, index])
-        for index, (middle, target) in enumerate(zip(passing, targets))
-    ]
-    for copy in arriving:
-        copy.start()
-    for before, copy in zip(arriving, leaving):
-        before.wait()
-        copy.start()
-    for copy in leaving:
-        copy.wait()
+    steps = []
+    for index in range(count):
+        rows = sources[index].shape[0]
+        pieces = PIECES if index < 2 else 1
+        for piece in range(pieces):
+            some = pl.ds(piece * (rows // pieces), rows // pieces)
+            place = len(steps)
+            steps.append((
+                pltpu.make_async_copy(sources[index].at[some], passing[index].at[some], sems.at[0, place]),
+                pltpu.make_async_copy(passing[index].at[some], targets[index].at[some], sems.at[1, place]),
+            ))
+    for arriving, _ in steps:
+        arriving.start()
+    for arriving, leaving in steps:
+        arriving.wait()
+        leaving.start()
+    for _, leaving in steps:
+        leaving.wait()
 
 
 def handed_on(arrays):
@@ -991,7 +999,7 @@
         in_specs=[any_spec] * count,
         out_specs=[any_spec] * count,
         scratch_shapes=[pltpu.VMEM(array.shape, array.dtype) for array in arrays]
-        + [pltpu.SemaphoreType.DMA((2, count))],
+        + [pltpu.SemaphoreType.DMA((2, count + 2 * (PIECES - 1)))],
         name="hand_on",
     )(*arrays)
 

time: 146 us -> 146 us (level)
  no operation moved by 1% of the time
where the time goes in v1:
time: 146 us; the launch traced here: 145 us
  Pallas kernels  145 us (99%)
    pallas_call x1, Pallas kernels, layer(): pl.pallas_call(functools.partial(layer_kernel, sizes, tuple(inputs), tupl...  141 us
    pallas_call x1, Pallas kernels, handed_on(): pl.pallas_call(functools.partial(hand_on_kernel, count), out_shape=[jax.S...  3.19 us

profile of v1, /device:TPU:0, one launch (start us, length us, event | category | flops | bytes accessed | tf_op | source)
XLA Modules:
  0.0 145.4 jit_solution(2063147232150211881)
XLA Ops:
  0.6 141.4 %layer.1 = (bf16[256,1024]{1,0:T(8,128)(2,1)}, f32[256,1024]{1,0:T(8,128)}, f32[8,128]{1,0:T(8,128)}, f32[8,128]{1,0:T(8,128)}, f32[256,128]{1,0:T(8,128)}, /*in...) custom-call(bf16[256,1024]{1,0:T(8,128)(2,1)} %bitcast.19, ...), custom_call_target="tpu_custom_call" | custom-call | tf_op jit(solution)/shard_map/layer/pallas_call | solution.py:953
  142.0 3.2 %hand_on.1 = (bf16[256,1024]{1,0:T(8,128)(2,1)}, f32[256,1024]{1,0:T(8,128)}, f32[8,128]{1,0:T(8,128)}, f32[8,128]{1,0:T(8,128)}, f32[256,128]{1,0:T(8,128)}, /*...) custom-call(bf16[256,1024]{1,0:T(8,128)(2,1)} %get-tuple-element.33., ...), custom_call_target="tpu_custom_call" | custom-call | tf_op jit(solution)/shard_map/hand_on/pallas_call | solution.py:996
